TPU v7x, 32 devices: a whole 2x2x4 slice. The times are simulated.
32 devices in a mesh: tm: 2 (over core), space: 16 (over z, y, x).
Axes of the slice: x: 2, y: 2, z: 4, core: 2. Of those that a mesh axis runs over, the one named last changes fastest.
Arguments:
- increment_start: float32 [2, 8, 512, 1024], P('tm', None, 'space'), may hold values from -6 to 6
- dual_model_start: float32 [2, 8, 512, 1024], P('tm', None, 'space'), may hold values from -6 to 6
- dual_obs_start: bfloat16 [2, 256, 128], P('tm', 'space'), may hold values from -6 to 6
- model_rhs: float32 [2, 8, 512, 1024], P('tm', None, 'space'), may hold values from -6 to 6
- err_var: float32 [2, 8, 512, 1024], P('tm', None, 'space'), may hold values from 0.2 to 2
- decays: float32 [2, 8, 512, 1024], P('tm', None, 'space'), may hold values from 0.1 to 0.95
- scaling: float32 [8, 512, 1024], P(None, 'space'), may hold values from 0.5 to 1
- diffusion: float32 [8], replicated, may hold values from 0.05 to 0.24
- owners: int32 [2, 256], P('tm', 'space'), may hold values from 0 to 15, as said below
- tile_cols: int32 [2, 256, 128], P('tm', 'space'), may hold values from 0 to 32767, as said below
- jacobian: bfloat16 [2, 256, 128, 1024], P('tm', 'space'), may hold values from -0.1875 to 0.1875
- innovation: bfloat16 [2, 256, 128], P('tm', 'space'), may hold values from -6 to 6
- obs_var: bfloat16 [2, 256, 128], P('tm', 'space'), may hold values from 0.5 to 4
Outputs:
- dual_model: float32 [2, 8, 512, 1024], P('tm', None, 'space')
- dual_obs: float32 [2, 256, 128], P('tm', 'space')
- increment: float32 [2, 8, 512, 1024], P('tm', None, 'space')
Inputs may be any that keep to these rules, and one draw needn't show every extreme that they name: `owners`: in each subwindow at most 2 of the 16 tiles of one device name the same owner, and one owner is named exactly 2 times by the tiles of every device. All 128 cells of a tile lie in one latitude row: tile_cols[k, t, c] // 1024 is the same for every c.
All inputs are finite; a program needn't handle non-finite values.
Results may differ from a plain program's by a relative error of at most 0.0042.
The roundings to bfloat16 on the way count: a program that leaves them out, or rounds other values in their place, can miss the bound.
Values may be sent and summed in bfloat16 or wider, within the bound.
A program may use at most 256 MiB of HBM per device.

v0:
```python
import math

import jax
import jax.numpy as jnp
from jax import lax
from jax.sharding import PartitionSpec as P

SUBSTEPS = 2
ITERS = 2


def with_halo(cells, sides, width):
    for axis, dim in sides:
        count = lax.axis_size(axis)
        ends = count - 1
        head = lax.slice_in_dim(cells, 0, width, axis=dim)
        tail = lax.slice_in_dim(cells, cells.shape[dim] - width, cells.shape[dim], axis=dim)
        cells = jnp.concatenate(
            [
                lax.ppermute(tail, axis, [(i, (i + 1) % count) for i in range(ends)]),
                cells,
                lax.ppermute(head, axis, [((i + 1) % count, i) for i in range(ends)]),
            ],
            axis=dim,
        )
    return cells


def shifted(value, axis, by):
    length = lax.axis_size(axis)
    pairs = [(i, i + by) for i in range(length) if 0 <= i + by < length]
    return lax.ppermute(value, axis, pairs)


def split_cells(cell_index, col_count):
    slots = cell_index.shape[0]
    block = math.gcd(slots, 8)
    row_ids = (cell_index[:, 0] // col_count).reshape(slots // block, block)
    col_ids = (cell_index % col_count).reshape(slots // block, block, cell_index.shape[1])
    return (block, row_ids, col_ids)


def pick_columns(fields, cell_index):
    levels, row_count, col_count = fields.shape
    slots = cell_index.shape[0]
    block, row_ids, col_ids = split_cells(cell_index, col_count)
    rounded = fields.astype(jnp.bfloat16)
    row_range = jnp.arange(row_count, dtype=jnp.int32)
    col_range = jnp.arange(col_count, dtype=jnp.int32)

    def pick_per_block(operands):
        rows_here, cols_here = operands
        row_onehot = (rows_here[:, None] == row_range[None, :]).astype(jnp.bfloat16)
        lines = jnp.einsum(
            "sr,lrc->slc", row_onehot, rounded, preferred_element_type=jnp.float32
        ).astype(jnp.bfloat16)
        col_onehot = (cols_here[:, :, None] == col_range[None, None, :]).astype(jnp.bfloat16)
        picked = jnp.einsum("stc,slc->stl", col_onehot, lines, preferred_element_type=jnp.float32)
        return picked.astype(jnp.bfloat16).reshape(block, -1)

    return lax.map(pick_per_block, (row_ids, col_ids)).reshape(slots, -1)


def spread_columns(contrib, cell_index, levels, row_count, col_count):
    slots, touched = cell_index.shape
    block, row_ids, col_ids = split_cells(cell_index, col_count)
    values = contrib.reshape(slots // block, block, touched, levels)
    row_range = jnp.arange(row_count, dtype=jnp.int32)
    col_range = jnp.arange(col_count, dtype=jnp.int32)

    def spread_per_block(total, operands):
        rows_here, cols_here, vals = operands
        col_onehot = (cols_here[:, :, None] == col_range[None, None, :]).astype(jnp.bfloat16)
        lines = jnp.einsum("stc,stl->slc", col_onehot, vals, preferred_element_type=jnp.float32)
        row_onehot = (rows_here[:, None] == row_range[None, :]).astype(jnp.float32)
        added = jnp.einsum("sr,slc->lrc", row_onehot, lines, precision=lax.Precision.HIGHEST)
        return (total + added, None)

    start = jnp.zeros((levels, row_count, col_count), jnp.float32)
    summed, unused = lax.scan(spread_per_block, start, (row_ids, col_ids, values))
    return summed


def obs_forward(jacobian_rows, gathered):
    return jnp.einsum("soj,sj->so", jacobian_rows, gathered, preferred_element_type=jnp.float32)


def obs_adjoint(jacobian_rows, obs_dual):
    summed = jnp.einsum(
        "soj,so->sj",
        jacobian_rows,
        obs_dual.astype(jnp.bfloat16),
        preferred_element_type=jnp.float32,
    )
    return summed.astype(jnp.bfloat16)


def pack_slots(values, position, owners_count, capacity, fill_value):
    buffer = jnp.full((owners_count * capacity,) + values.shape[1:], fill_value, values.dtype)
    return buffer.at[position].set(values).reshape((owners_count, capacity) + values.shape[1:])


def on_device(
    increment_start,
    dual_model_start,
    dual_obs_start,
    model_rhs,
    err_var,
    decays,
    scaling,
    diffusion,
    owners,
    tile_cols,
    jacobian,
    innovation,
    obs_var,
):
    increment = increment_start[0]
    dual_model = dual_model_start[0]
    rhs_field = model_rhs[0]
    err_field = err_var[0]
    decay_field = decays[0]
    owner_list = owners[0]
    cell_index = tile_cols[0]
    jac_tiles = jacobian[0]
    observed = innovation[0].astype(jnp.float32)
    obs_error = obs_var[0].astype(jnp.float32)
    obs_dual = dual_obs_start[0].astype(jnp.float32)
    levels, row_count, col_count = increment.shape
    tiles_here = owner_list.shape[0]
    owners_count = lax.axis_size("space")
    capacity = max(2, 2 * tiles_here // owners_count)
    slots_all = owners_count * capacity
    diff_coef = diffusion[:, None, None]
    one_hot = (owner_list[:, None] == jnp.arange(owners_count, dtype=jnp.int32)[None, :]).astype(
        jnp.int32
    )
    earlier_count = jnp.cumsum(one_hot, axis=0) - one_hot
    slot_rank = jnp.sum(earlier_count * one_hot, axis=1)
    position = owner_list * capacity + slot_rank
    requests = lax.all_to_all(
        pack_slots(cell_index, position, owners_count, capacity, 0),
        "space",
        split_axis=0,
        concat_axis=0,
        tiled=True,
    ).reshape(slots_all, -1)
    for repeat in range(ITERS):
        beside_all = with_halo(jnp.stack([dual_model, increment]), (("tm", 0),), 1)
        current = beside_all[::3]
        for apply_repeat in range(SUBSTEPS):
            scaled = scaling * current
            padded = with_halo(scaled, (("space", 2),), 1)
            laplace = (
                padded[:, :, 2:]
                + padded[:, :, :-2]
                + jnp.roll(scaled, 1, 3)
                + jnp.roll(scaled, -1, 3)
                - 4.0 * scaled
            )
            current = scaling * (scaled + diff_coef * laplace)
        wanted = pick_columns(increment, requests).reshape(owners_count, capacity, -1)
        sent_grad = pack_slots(
            obs_adjoint(jac_tiles, obs_dual), position, owners_count, capacity, 0.0
        )
        got_cols, got_grad = (
            lax.all_to_all(wanted, "space", split_axis=0, concat_axis=0, tiled=True),
            lax.all_to_all(sent_grad, "space", split_axis=0, concat_axis=0, tiled=True),
        )
        own_cols = got_cols.reshape(slots_all, -1)[position]
        obs_image = obs_forward(jac_tiles, own_cols)
        adjoint_field = spread_columns(
            got_grad.reshape(slots_all, -1), requests, levels, row_count, col_count
        )
        obs_dual = obs_dual + (observed - obs_error * obs_dual - obs_image) / obs_error
        r_model = rhs_field - err_field * dual_model - (increment - current[0])
        r_dual = -(dual_model - current[1]) - adjoint_field
        upward = r_dual
        upward = r_dual + shifted(decay_field * upward, "tm", -1)
        source = r_model - err_field * upward
        along = source
        along = source + decay_field * shifted(along, "tm", 1)
        dual_model = dual_model + upward
        increment = increment + along
    return (dual_model[None], obs_dual[None], increment[None])


def solution(mesh):
    in_specs = (
        P("tm", None, "space", None),
        P("tm", None, "space", None),
        P("tm", "space", None),
        P("tm", None, "space", None),
        P("tm", None, "space", None),
        P("tm", None, "space", None),
        P(None, "space", None),
        P(),
        P("tm", "space"),
        P("tm", "space", None),
        P("tm", "space", None, None),
        P("tm", "space", None),
        P("tm", "space", None),
    )
    out_specs = (P("tm", None, "space", None), P("tm", "space", None), P("tm", None, "space", None))
    return jax.shard_map(
        on_device, mesh=mesh, in_specs=in_specs, out_specs=out_specs, check_vma=False
    )
```

profile of v0, /device:TPU:9, one launch (start us, length us, event | category | flops | bytes accessed | tf_op | source)
XLA Modules:
  0.0 197.3 jit_solution(862586723636953394)
XLA Ops:
  0.6 1.3 collective-permute-start
  1.9 5.0 %collective-permute-start.1 = (f32[1,8,32,1024]{3,2,1,0:T(8,128)}, f32[1,8,32,1024]{3,2,1,0:T(8,128)}, u32[]{:S(2)}, u32[]{:S(2)}) collective-permute-start(f32[1,8,32,1024]{3,2,1,0:T(8,128)} %param.22), channel_id=1, source_target_pairs={{16,0},{17,1},{18,2},{19,3},{20,4},{21,5},{22,6},{23,7},{24,8},{25... | collective-permute-start | bytes 3145736 | tf_op jit(solution)/shard_map/ppermute | solution.py:22
  10.4 6.7 %all-to-all-start.1 = ((s32[16,2,128]{2,1,0:T(2,128)}), s32[16,2,128]{2,1,0:T(2,128)S(1)}, u32[]{:S(2)}, u32[]{:S(2)}) async-start(s32[16,2,128]{2,1,0:T(2,128)} %bitcast.11), calls=%async_computation.1 | async-start | bytes 32768 | tf_op jit(solution)/shard_map/all_to_all | solution.py:141
  17.1 2.8 %fusion.60 = f32[16,1,1024]{2,1,0:T(1,128)S(1)} fusion(bf16[1,16,128,1024]{3,2,1,0:T(8,128)(2,1)} %param.31, bf16[16,128,1]{1,0,2:T(8,128)(2,1)} %bitcast.256), kind=kOutput, calls=%fused_computation.77 | convolution fusion | flops 4194304 | bytes 4263936 | tf_op jit(solution)/shard_map/soj,so->sj/dot_general | solution.py:89
  22.2 5.5 %all-to-all-start = ((bf16[16,2,1024]{2,1,0:T(2,128)(2,1)}), bf16[16,2,1024]{2,1,0:T(2,128)(2,1)S(1)}, u32[]{:S(2)}, u32[]{:S(2)}) async-start(bf16[16,2,1024]{2,1,0:T(2,128)(2,1)} %reshape.99), calls=%async_computation | async-start | bytes 131072 | tf_op jit(solution)/shard_map/all_to_all | solution.py:168
  27.9 5.4 %all-to-all-done = bf16[16,2,1024]{2,1,0:T(2,128)(2,1)S(1)} async-done(((bf16[16,2,1024]{2,1,0:T(2,128)(2,1)}), bf16[16,2,1024]{2,1,0:T(2,128)(2,1)S(1)}, u32[]{:S(2)}, u32[]{:S(2)}) %all-to-all-start) | async-done | bytes 65568 | tf_op jit(solution)/shard_map/all_to_all | solution.py:168
  34.8 7.0 %while.46 = (s32[]{:T(128)}, f32[8,32,1024]{2,1,0:T(8,128)S(1)}, bf16[4,8,128,8]{2,3,1,0:T(8,128)(2,1)S(1)}, s32[4,8,128]{2,1,0:T(8,128)S(1)}, s32[4,8]{1,0:T(4,128)S(1)}, /*index=5*/s32[]{:T(128)}, s32[]{:T(128)}) while((s32[]{:T(128)}, f32[8,32,1024]{2,1,0:T(8,128)S(1)}, bf16[4,8,128,8]{2,3,1,0:T(8,128)(2,1)S(1)}, ...), condition=%wide.region_5.6_spmd.clone, body=%wide.region_4.5_spmd.clone.sunk | while | flops 43516160 | bytes 2650307 | solution.py:80
  41.8 2.3 %pad_maximum_fusion = f32[4,8,32,1024]{3,2,1,0:T(8,128)S(1)} fusion(f32[1,8,32,1024]{3,2,1,0:T(8,128)} %collective-permute-done.1, f32[1,8,32,1024]{3,2,1,0:T(8,128)S(1)} %copy-done.8, f32[1,8,32,1024]{3,2,1,0:T(8,128)} %param.22, f32[1,8,32,1024]{3,2,1,0:T(8,128)} %collective-permute-done), kind=kLoop, calls=%fused_computation.69 | loop fusion | flops 3145728 | bytes 8388608 | tf_op jit(solution)/shard_map/concatenate | solution.py:18
  45.4 3.1 %collective-permute-start.2 = (f32[2,8,1,1024]{3,2,1,0:T(1,128)S(1)}, f32[2,8,1,1024]{3,2,1,0:T(1,128)S(1)}, u32[]{:S(2)}, u32[]{:S(2)}) collective-permute-start(f32[2,8,1,1024]{3,2,1,0:T(1,128)S(1)} %get-tuple-element.313), channel_id=1, source_target_pairs={{1,0},{2,1},{3,2},{4,3},{5,4},{6,5},{7,6},{8,7},{9,8},{10,9},{11,1... | collective-permute-start | bytes 196616 | tf_op jit(solution)/shard_map/ppermute | solution.py:22
  48.5 2.2 %collective-permute-start.3 = (f32[2,8,1,1024]{3,2,1,0:T(1,128)S(1)}, f32[2,8,1,1024]{3,2,1,0:T(1,128)S(1)}, u32[]{:S(2)}, u32[]{:S(2)}) collective-permute-start(f32[2,8,1,1024]{3,2,1,0:T(1,128)S(1)} %get-tuple-element.314), channel_id=1, source_target_pairs={{0,1},{1,2},{2,3},{3,4},{4,5},{5,6},{6,7},{7,8},{8,9},{9,10},{10,1... | collective-permute-start | bytes 196616 | tf_op jit(solution)/shard_map/ppermute | solution.py:20
  50.9 4.4 %collective-permute-done.3 = f32[2,8,1,1024]{3,2,1,0:T(1,128)S(1)} collective-permute-done((f32[2,8,1,1024]{3,2,1,0:T(1,128)S(1)}, f32[2,8,1,1024]{3,2,1,0:T(1,128)S(1)}, u32[]{:S(2)}, u32[]{:S(2)}) %collective-permute-start.3) | collective-permute-done | bytes 65568 | tf_op jit(solution)/shard_map/ppermute | solution.py:20
  55.3 1.6 fusion.91
  57.9 1.9 collective-permute-start.4
  59.9 3.4 %collective-permute-start.5 = (f32[2,8,1,1024]{3,2,1,0:T(1,128)S(1)}, f32[2,8,1,1024]{3,2,1,0:T(1,128)S(1)}, u32[]{:S(2)}, u32[]{:S(2)}) collective-permute-start(f32[2,8,1,1024]{3,2,1,0:T(1,128)S(1)} %get-tuple-element.308), channel_id=1, source_target_pairs={{0,1},{1,2},{2,3},{3,4},{4,5},{5,6},{6,7},{7,8},{8,9},{9,10},{10,1... | collective-permute-start | bytes 196616 | tf_op jit(solution)/shard_map/ppermute | solution.py:20
  63.4 3.3 %collective-permute-done.5 = f32[2,8,1,1024]{3,2,1,0:T(1,128)S(1)} collective-permute-done((f32[2,8,1,1024]{3,2,1,0:T(1,128)S(1)}, f32[2,8,1,1024]{3,2,1,0:T(1,128)S(1)}, u32[]{:S(2)}, u32[]{:S(2)}) %collective-permute-start.5) | collective-permute-done | bytes 65568 | tf_op jit(solution)/shard_map/ppermute | solution.py:20
  66.7 1.5 fusion.83
  68.2 1.6 bitcast_multiply_fusion.7
  69.9 5.7 %collective-permute-start.6 = (f32[8,32,1024]{2,1,0:T(8,128)}, f32[8,32,1024]{2,1,0:T(8,128)}, u32[]{:S(2)}, u32[]{:S(2)}) collective-permute-start(f32[8,32,1024]{2,1,0:T(8,128)} %bitcast_multiply_fusion.7), channel_id=1, source_target_pairs={{16,0},{17,1},{18,2},{19,3},{20,4},{21,5},{22,6},{23,7},{24,8},{25... | collective-permute-start | bytes 3145736 | tf_op jit(solution)/shard_map/ppermute | solution.py:32
  77.2 5.5 %fusion.100 = (f32[8,32,1024]{2,1,0:T(8,128)}, f32[8,32,1024]{2,1,0:T(8,128)}) fusion(f32[2,8,32,1024]{3,2,1,0:T(8,128)} %copy-done.9, f32[1,8,32,1024]{3,2,1,0:T(8,128)} %param.25, f32[1,8,32,1024]{3,2,1,0:T(8,128)} %param.24, f32[1,8,32,1024]{3,2,1,0:T(8,128)} %param.21, f32[1,8,32,1024]{3,2,1,0:T(8,128)} %param.22, ...), kind=kLoop, calls=%fused_computation.130 | loop fusion | flops 2883584 | bytes 10485760 | tf_op jit(solution)/shard_map/sub | solution.py:180
  84.0 6.7 %while.44 = (s32[]{:T(128)}, bf16[4,8,1024]{2,1,0:T(8,128)(2,1)S(1)}, s32[4,8,128]{2,1,0:T(8,128)S(1)}, s32[4,8]{1,0:T(4,128)S(1)}, bf16[8,32,1024]{2,1,0:T(8,128)(2,1)S(1)}, /*index=5*/s32[]{:T(128)}) while((s32[]{:T(128)}, bf16[4,8,1024]{2,1,0:T(8,128)(2,1)S(1)}, s32[4,8,128]{2,1,0:T(8,128)S(1)}, s32[4,8]{1,0:T(4,128)S(1)}, ...), condition=%wide.region_7.8_spmd.clone, body=%wide.region_6.7_spmd.clone.sunk | while | flops 22094080 | bytes 913585 | solution.py:61
  91.3 3.6 %all-to-all-start.2 = ((bf16[16,2,1024]{2,1,0:T(2,128)(2,1)}), bf16[16,2,1024]{2,1,0:T(2,128)(2,1)S(1)}, u32[]{:S(2)}, u32[]{:S(2)}) async-start(bf16[16,2,1024]{2,1,0:T(2,128)(2,1)} %reshape_reshape.13), calls=%async_computation.2 | async-start | bytes 131072 | tf_op jit(solution)/shard_map/all_to_all | solution.py:167
  94.9 4.9 %all-to-all-done.2 = bf16[16,2,1024]{2,1,0:T(2,128)(2,1)S(1)} async-done(((bf16[16,2,1024]{2,1,0:T(2,128)(2,1)}), bf16[16,2,1024]{2,1,0:T(2,128)(2,1)S(1)}, u32[]{:S(2)}, u32[]{:S(2)}) %all-to-all-start.2) | async-done | bytes 65568 | tf_op jit(solution)/shard_map/all_to_all | solution.py:167
  100.5 3.7 %fusion.130 = (bf16[8,32,1024]{2,1,0:T(8,128)(2,1)S(1)}, f32[8,32,1024]{2,1,0:T(8,128)}) fusion(f32[8,32,1024]{2,1,0:T(8,128)} %get-tuple-element.289, f32[8,32,1024]{2,1,0:T(8,128)} %collective-permute-done.7, f32[1,8,32,1024]{3,2,1,0:T(8,128)} %param.26, f32[1,8,32,1024]{3,2,1,0:T(8,128)} %param.21), kind=kLoop, calls=%fused_computation.197 | loop fusion | flops 1048576 | bytes 5767168 | tf_op jit(solution)/shard_map/convert_element_type | solution.py:47
  104.2 6.7 %while.45 = (s32[]{:T(128)}, bf16[4,8,1024]{2,1,0:T(8,128)(2,1)S(1)}, s32[4,8,128]{2,1,0:T(8,128)S(1)}, s32[4,8]{1,0:T(4,128)S(1)}, bf16[8,32,1024]{2,1,0:T(8,128)(2,1)S(1)}, /*index=5*/s32[]{:T(128)}) while((s32[]{:T(128)}, bf16[4,8,1024]{2,1,0:T(8,128)(2,1)S(1)}, s32[4,8,128]{2,1,0:T(8,128)S(1)}, s32[4,8]{1,0:T(4,128)S(1)}, ...), condition=%wide.region_12.13_spmd.clone, body=%wide.region_11.12_spmd.clone.sunk | while | flops 22094080 | bytes 913585 | solution.py:61
  111.6 4.4 %all-to-all-start.4 = ((bf16[16,2,1024]{2,1,0:T(2,128)(2,1)}), bf16[16,2,1024]{2,1,0:T(2,128)(2,1)S(1)}, u32[]{:S(2)}, u32[]{:S(2)}) async-start(bf16[16,2,1024]{2,1,0:T(2,128)(2,1)} %reshape_reshape.15), calls=%async_computation.4 | async-start | bytes 131072 | tf_op jit(solution)/shard_map/all_to_all | solution.py:167
  116.0 3.4 %fusion.58 = f32[16,1,128]{2,1,0:T(1,128)S(1)} fusion(bf16[1,16,128,1024]{3,2,1,0:T(8,128)(2,1)} %param.31, bf16[16,1024,1]{1,0,2:T(8,128)(2,1)S(1)} %bitcast.252), kind=kOutput, calls=%fused_computation.75 | convolution fusion | flops 4194304 | bytes 4235264 | tf_op jit(solution)/shard_map/soj,sj->so/dot_general | solution.py:85
  119.3 2.1 %all-to-all-done.4 = bf16[16,2,1024]{2,1,0:T(2,128)(2,1)S(1)} async-done(((bf16[16,2,1024]{2,1,0:T(2,128)(2,1)}), bf16[16,2,1024]{2,1,0:T(2,128)(2,1)S(1)}, u32[]{:S(2)}, u32[]{:S(2)}) %all-to-all-start.4) | async-done | bytes 65568 | tf_op jit(solution)/shard_map/all_to_all | solution.py:167
  122.1 3.5 %fusion.54 = f32[16,1,128]{2,1,0:T(1,128)S(1)} fusion(bf16[1,16,128,1024]{3,2,1,0:T(8,128)(2,1)} %param.31, bf16[16,1024,1]{1,0,2:T(8,128)(2,1)S(1)} %bitcast.253), kind=kOutput, calls=%fused_computation.71 | convolution fusion | flops 4194304 | bytes 4235264 | tf_op jit(solution)/shard_map/soj,sj->so/dot_general | solution.py:85
  128.3 4.4 %all-to-all-start.3 = ((bf16[16,2,1024]{2,1,0:T(2,128)(2,1)}), bf16[16,2,1024]{2,1,0:T(2,128)(2,1)S(1)}, u32[]{:S(2)}, u32[]{:S(2)}) async-start(bf16[16,2,1024]{2,1,0:T(2,128)(2,1)} %reshape.104), calls=%async_computation.3 | async-start | bytes 131072 | tf_op jit(solution)/shard_map/all_to_all | solution.py:168
  132.7 7.9 %collective-permute-start.9 = (f32[1,8,32,1024]{3,2,1,0:T(8,128)S(1)}, f32[1,8,32,1024]{3,2,1,0:T(8,128)}, u32[]{:S(2)}, u32[]{:S(2)}) collective-permute-start(f32[1,8,32,1024]{3,2,1,0:T(8,128)S(1)} %bitcast.248), channel_id=1, source_target_pairs={{16,0},{17,1},{18,2},{19,3},{20,4},{21,5},{22,6},{23,7},{24,8},{25... | collective-permute-start | bytes 3145736 | tf_op jit(solution)/shard_map/ppermute | solution.py:22
  141.9 2.2 %reshape_reshape.14 = bf16[4,8,128,8]{3,2,1,0:T(8,128)(2,1)} reshape(bf16[16,2,1024]{2,1,0:T(2,128)(2,1)S(1)} %all-to-all-done.3) | data formatting | bytes 131072 | tf_op jit(solution)/shard_map/reshape;reshape | solution.py:67
  144.1 1.5 copy.28
  145.6 6.9 %while.47 = (s32[]{:T(128)}, f32[8,32,1024]{2,1,0:T(8,128)S(1)}, bf16[4,8,128,8]{2,3,1,0:T(8,128)(2,1)S(1)}, s32[4,8,128]{2,1,0:T(8,128)S(1)}, s32[4,8]{1,0:T(4,128)S(1)}, /*index=5*/s32[]{:T(128)}, s32[]{:T(128)}) while((s32[]{:T(128)}, f32[8,32,1024]{2,1,0:T(8,128)S(1)}, bf16[4,8,128,8]{2,3,1,0:T(8,128)(2,1)S(1)}, ...), condition=%wide.region_10.11_spmd.clone, body=%wide.region_9.10_spmd.clone.sunk | while | flops 43516160 | bytes 2650307 | solution.py:80
  152.6 2.2 %pad_maximum_fusion.1 = f32[4,8,32,1024]{3,2,1,0:T(8,128)S(1)} fusion(f32[1,8,32,1024]{3,2,1,0:T(8,128)} %collective-permute-done.9, f32[1,8,32,1024]{3,2,1,0:T(8,128)} %bitcast.251, f32[1,8,32,1024]{3,2,1,0:T(8,128)S(1)} %bitcast.249, f32[1,8,32,1024]{3,2,1,0:T(8,128)} %collective-permute-done.8), kind=kLoop, calls=%fused_computation.70 | loop fusion | flops 3145728 | bytes 8388608 | tf_op jit(solution)/shard_map/concatenate | solution.py:18
  156.1 4.0 %collective-permute-start.10 = (f32[2,8,1,1024]{3,2,1,0:T(1,128)S(1)}, f32[2,8,1,1024]{3,2,1,0:T(1,128)S(1)}, u32[]{:S(2)}, u32[]{:S(2)}) collective-permute-start(f32[2,8,1,1024]{3,2,1,0:T(1,128)S(1)} %get-tuple-element.301), channel_id=1, source_target_pairs={{1,0},{2,1},{3,2},{4,3},{5,4},{6,5},{7,6},{8,7},{9,8},{10,9},{11,1... | collective-permute-start | bytes 196616 | tf_op jit(solution)/shard_map/ppermute | solution.py:22
  160.1 1.9 collective-permute-start.11
  162.2 4.7 %collective-permute-done.11 = f32[2,8,1,1024]{3,2,1,0:T(1,128)S(1)} collective-permute-done((f32[2,8,1,1024]{3,2,1,0:T(1,128)S(1)}, f32[2,8,1,1024]{3,2,1,0:T(1,128)S(1)}, u32[]{:S(2)}, u32[]{:S(2)}) %collective-permute-start.11) | collective-permute-done | bytes 65568 | tf_op jit(solution)/shard_map/ppermute | solution.py:20
  166.9 1.6 fusion.76
  169.4 1.9 collective-permute-start.12
  171.3 3.6 %collective-permute-start.13 = (f32[2,8,1,1024]{3,2,1,0:T(1,128)S(1)}, f32[2,8,1,1024]{3,2,1,0:T(1,128)S(1)}, u32[]{:S(2)}, u32[]{:S(2)}) collective-permute-start(f32[2,8,1,1024]{3,2,1,0:T(1,128)S(1)} %get-tuple-element.296), channel_id=1, source_target_pairs={{0,1},{1,2},{2,3},{3,4},{4,5},{5,6},{6,7},{7,8},{8,9},{9,10},{10,1... | collective-permute-start | bytes 196616 | tf_op jit(solution)/shard_map/ppermute | solution.py:20
  175.1 3.2 %collective-permute-done.13 = f32[2,8,1,1024]{3,2,1,0:T(1,128)S(1)} collective-permute-done((f32[2,8,1,1024]{3,2,1,0:T(1,128)S(1)}, f32[2,8,1,1024]{3,2,1,0:T(1,128)S(1)}, u32[]{:S(2)}, u32[]{:S(2)}) %collective-permute-start.13) | collective-permute-done | bytes 65568 | tf_op jit(solution)/shard_map/ppermute | solution.py:20
  178.2 1.6 fusion.68
  180.3 6.7 %collective-permute-start.14 = (f32[8,32,1024]{2,1,0:T(8,128)S(1)}, f32[8,32,1024]{2,1,0:T(8,128)S(1)}, u32[]{:S(2)}, u32[]{:S(2)}) collective-permute-start(f32[8,32,1024]{2,1,0:T(8,128)S(1)} %bitcast_multiply_fusion.5), channel_id=1, source_target_pairs={{16,0},{17,1},{18,2},{19,3},{20,4},{21,5},{22,6},{23,7},{24,8},{25... | collective-permute-start | bytes 3145736 | tf_op jit(solution)/shard_map/ppermute | solution.py:32
  187.0 2.2 %collective-permute-done.14 = f32[8,32,1024]{2,1,0:T(8,128)S(1)} collective-permute-done((f32[8,32,1024]{2,1,0:T(8,128)S(1)}, f32[8,32,1024]{2,1,0:T(8,128)S(1)}, u32[]{:S(2)}, u32[]{:S(2)}) %collective-permute-start.14) | collective-permute-done | bytes 1048608 | tf_op jit(solution)/shard_map/ppermute | solution.py:32
  189.2 2.0 fusion.94
  191.2 1.4 collective-permute-start.15
  192.6 3.3 %collective-permute-done.15 = f32[8,32,1024]{2,1,0:T(8,128)S(1)} collective-permute-done((f32[8,32,1024]{2,1,0:T(8,128)S(1)}, f32[8,32,1024]{2,1,0:T(8,128)S(1)}, u32[]{:S(2)}, u32[]{:S(2)}) %collective-permute-start.15) | collective-permute-done | bytes 1048608 | tf_op jit(solution)/shard_map/ppermute | solution.py:32
  195.9 1.4 fusion.109
  (180 shorter events, 49.0 us)
Async XLA Ops:
  0.6 8.6 %copy-start = (s32[1,16,128]{2,1,0:T(8,128)S(1)}, s32[1,16,128]{2,1,0:T(8,128)}, u32[]{:S(2)}) copy-start(s32[1,16,128]{2,1,0:T(8,128)} %param.30) | copy-start | bytes 24580
  0.6 41.1 %collective-permute-start = (f32[1,8,32,1024]{3,2,1,0:T(8,128)}, f32[1,8,32,1024]{3,2,1,0:T(8,128)}, u32[]{:S(2)}, u32[]{:S(2)}) collective-permute-start(f32[1,8,32,1024]{3,2,1,0:T(8,128)} %param.21), channel_id=1, source_target_pairs={{0,16},{1,17},{2,18},{3,19},{4,20},{5,21},{6,22},{7,23},{8,24},{9,... | collective-permute-start | bytes 3145736 | tf_op jit(solution)/shard_map/ppermute | solution.py:20
  1.9 39.9 %collective-permute-start.1 = (f32[1,8,32,1024]{3,2,1,0:T(8,128)}, f32[1,8,32,1024]{3,2,1,0:T(8,128)}, u32[]{:S(2)}, u32[]{:S(2)}) collective-permute-start(f32[1,8,32,1024]{3,2,1,0:T(8,128)} %param.22), channel_id=1, source_target_pairs={{16,0},{17,1},{18,2},{19,3},{20,4},{21,5},{22,6},{23,7},{24,8},{25... | collective-permute-start | bytes 3145736 | tf_op jit(solution)/shard_map/ppermute | solution.py:22
  10.4 11.8 %all-to-all-start.1 = ((s32[16,2,128]{2,1,0:T(2,128)}), s32[16,2,128]{2,1,0:T(2,128)S(1)}, u32[]{:S(2)}, u32[]{:S(2)}) async-start(s32[16,2,128]{2,1,0:T(2,128)} %bitcast.11), calls=%async_computation.1 | async-start | bytes 32768 | tf_op jit(solution)/shard_map/all_to_all | solution.py:141
  22.2 11.1 %all-to-all-start = ((bf16[16,2,1024]{2,1,0:T(2,128)(2,1)}), bf16[16,2,1024]{2,1,0:T(2,128)(2,1)S(1)}, u32[]{:S(2)}, u32[]{:S(2)}) async-start(bf16[16,2,1024]{2,1,0:T(2,128)(2,1)} %reshape.99), calls=%async_computation | async-start | bytes 131072 | tf_op jit(solution)/shard_map/all_to_all | solution.py:168
  34.8 7.0 %copy-start.8 = (f32[1,8,32,1024]{3,2,1,0:T(8,128)S(1)}, f32[1,8,32,1024]{3,2,1,0:T(8,128)}, u32[]{:S(2)}) copy-start(f32[1,8,32,1024]{3,2,1,0:T(8,128)} %param.21) | copy-start | bytes 3145732
  41.8 2.4 %copy-start.3 = (f32[8,32,1024]{2,1,0:T(8,128)S(1)}, f32[8,32,1024]{2,1,0:T(8,128)}, u32[]{:S(2)}) copy-start(f32[8,32,1024]{2,1,0:T(8,128)} %param.27) | copy-start | bytes 3145732
  44.5 10.9 %copy-start.14 = (f32[8]{0:T(128)S(1)}, f32[8]{0:T(128)}, u32[]{:S(2)}) copy-start(f32[8]{0:T(128)} %param.28) | copy-start | bytes 100
  45.4 5.4 %collective-permute-start.2 = (f32[2,8,1,1024]{3,2,1,0:T(1,128)S(1)}, f32[2,8,1,1024]{3,2,1,0:T(1,128)S(1)}, u32[]{:S(2)}, u32[]{:S(2)}) collective-permute-start(f32[2,8,1,1024]{3,2,1,0:T(1,128)S(1)} %get-tuple-element.313), channel_id=1, source_target_pairs={{1,0},{2,1},{3,2},{4,3},{5,4},{6,5},{7,6},{8,7},{9,8},{10,9},{11,1... | collective-permute-start | bytes 196616 | tf_op jit(solution)/shard_map/ppermute | solution.py:22
  48.5 6.8 %collective-permute-start.3 = (f32[2,8,1,1024]{3,2,1,0:T(1,128)S(1)}, f32[2,8,1,1024]{3,2,1,0:T(1,128)S(1)}, u32[]{:S(2)}, u32[]{:S(2)}) collective-permute-start(f32[2,8,1,1024]{3,2,1,0:T(1,128)S(1)} %get-tuple-element.314), channel_id=1, source_target_pairs={{0,1},{1,2},{2,3},{3,4},{4,5},{5,6},{6,7},{7,8},{8,9},{9,10},{10,1... | collective-permute-start | bytes 196616 | tf_op jit(solution)/shard_map/ppermute | solution.py:20
  57.9 5.4 %collective-permute-start.4 = (f32[2,8,1,1024]{3,2,1,0:T(1,128)S(1)}, f32[2,8,1,1024]{3,2,1,0:T(1,128)S(1)}, u32[]{:S(2)}, u32[]{:S(2)}) collective-permute-start(f32[2,8,1,1024]{3,2,1,0:T(1,128)S(1)} %get-tuple-element.307), channel_id=1, source_target_pairs={{1,0},{2,1},{3,2},{4,3},{5,4},{6,5},{7,6},{8,7},{9,8},{10,9},{11,1... | collective-permute-start | bytes 196616 | tf_op jit(solution)/shard_map/ppermute | solution.py:22
  59.9 6.8 %collective-permute-start.5 = (f32[2,8,1,1024]{3,2,1,0:T(1,128)S(1)}, f32[2,8,1,1024]{3,2,1,0:T(1,128)S(1)}, u32[]{:S(2)}, u32[]{:S(2)}) collective-permute-start(f32[2,8,1,1024]{3,2,1,0:T(1,128)S(1)} %get-tuple-element.308), channel_id=1, source_target_pairs={{0,1},{1,2},{2,3},{3,4},{4,5},{5,6},{6,7},{7,8},{8,9},{9,10},{10,1... | collective-permute-start | bytes 196616 | tf_op jit(solution)/shard_map/ppermute | solution.py:20
  66.7 1.6 copy-start.4
  66.7 1.6 copy-start.10
  68.2 1.7 copy-start.9
  69.9 7.3 %collective-permute-start.6 = (f32[8,32,1024]{2,1,0:T(8,128)}, f32[8,32,1024]{2,1,0:T(8,128)}, u32[]{:S(2)}, u32[]{:S(2)}) collective-permute-start(f32[8,32,1024]{2,1,0:T(8,128)} %bitcast_multiply_fusion.7), channel_id=1, source_target_pairs={{16,0},{17,1},{18,2},{19,3},{20,4},{21,5},{22,6},{23,7},{24,8},{25... | collective-permute-start | bytes 3145736 | tf_op jit(solution)/shard_map/ppermute | solution.py:32
  82.7 17.8 %collective-permute-start.7 = (f32[8,32,1024]{2,1,0:T(8,128)}, f32[8,32,1024]{2,1,0:T(8,128)}, u32[]{:S(2)}, u32[]{:S(2)}) collective-permute-start(f32[8,32,1024]{2,1,0:T(8,128)} %get-tuple-element.289), channel_id=1, source_target_pairs={{0,16},{1,17},{2,18},{3,19},{4,20},{5,21},{6,22},{7,23},{8,24},{9,... | collective-permute-start | bytes 3145736 | tf_op jit(solution)/shard_map/ppermute | solution.py:32
  91.3 8.5 %all-to-all-start.2 = ((bf16[16,2,1024]{2,1,0:T(2,128)(2,1)}), bf16[16,2,1024]{2,1,0:T(2,128)(2,1)S(1)}, u32[]{:S(2)}, u32[]{:S(2)}) async-start(bf16[16,2,1024]{2,1,0:T(2,128)(2,1)} %reshape_reshape.13), calls=%async_computation.2 | async-start | bytes 131072 | tf_op jit(solution)/shard_map/all_to_all | solution.py:167
  111.6 9.9 %all-to-all-start.4 = ((bf16[16,2,1024]{2,1,0:T(2,128)(2,1)}), bf16[16,2,1024]{2,1,0:T(2,128)(2,1)S(1)}, u32[]{:S(2)}, u32[]{:S(2)}) async-start(bf16[16,2,1024]{2,1,0:T(2,128)(2,1)} %reshape_reshape.15), calls=%async_computation.4 | async-start | bytes 131072 | tf_op jit(solution)/shard_map/all_to_all | solution.py:167
  122.1 3.6 %copy-start.13 = (bf16[1,16,128]{2,1,0:T(8,128)(2,1)S(1)}, bf16[1,16,128]{2,1,0:T(8,128)(2,1)}, u32[]{:S(2)}) copy-start(bf16[1,16,128]{2,1,0:T(8,128)(2,1)} %param.23) | copy-start | bytes 12292
  122.1 3.6 %copy-start.15 = (bf16[1,16,128]{2,1,0:T(8,128)(2,1)S(1)}, bf16[1,16,128]{2,1,0:T(8,128)(2,1)}, u32[]{:S(2)}) copy-start(bf16[1,16,128]{2,1,0:T(8,128)(2,1)} %param.33) | copy-start | bytes 12292
  122.1 3.6 %copy-start.16 = (bf16[1,16,128]{2,1,0:T(8,128)(2,1)S(1)}, bf16[1,16,128]{2,1,0:T(8,128)(2,1)}, u32[]{:S(2)}) copy-start(bf16[1,16,128]{2,1,0:T(8,128)(2,1)} %param.32) | copy-start | bytes 12292
  122.1 4.2 %copy-start.2 = (bf16[1,16,128,1024]{3,2,1,0:T(8,128)(2,1)S(1)}, bf16[1,16,128,1024]{3,2,1,0:T(8,128)(2,1)}, u32[]{:S(2)}) copy-start(bf16[1,16,128,1024]{3,2,1,0:T(8,128)(2,1)} %param.31) | copy-start | bytes 12582916
  126.3 6.4 %copy-start.6 = (f32[8,32,1024]{2,1,0:T(8,128)S(1)}, f32[8,32,1024]{2,1,0:T(8,128)}, u32[]{:S(2)}) copy-start(f32[8,32,1024]{2,1,0:T(8,128)} %get-tuple-element.290) | copy-start | bytes 3145732
  128.3 13.6 %all-to-all-start.3 = ((bf16[16,2,1024]{2,1,0:T(2,128)(2,1)}), bf16[16,2,1024]{2,1,0:T(2,128)(2,1)S(1)}, u32[]{:S(2)}, u32[]{:S(2)}) async-start(bf16[16,2,1024]{2,1,0:T(2,128)(2,1)} %reshape.104), calls=%async_computation.3 | async-start | bytes 131072 | tf_op jit(solution)/shard_map/all_to_all | solution.py:168
  132.7 19.8 %collective-permute-start.9 = (f32[1,8,32,1024]{3,2,1,0:T(8,128)S(1)}, f32[1,8,32,1024]{3,2,1,0:T(8,128)}, u32[]{:S(2)}, u32[]{:S(2)}) collective-permute-start(f32[1,8,32,1024]{3,2,1,0:T(8,128)S(1)} %bitcast.248), channel_id=1, source_target_pairs={{16,0},{17,1},{18,2},{19,3},{20,4},{21,5},{22,6},{23,7},{24,8},{25... | collective-permute-start | bytes 3145736 | tf_op jit(solution)/shard_map/ppermute | solution.py:22
  140.6 12.0 %collective-permute-start.8 = (f32[1,8,32,1024]{3,2,1,0:T(8,128)}, f32[1,8,32,1024]{3,2,1,0:T(8,128)}, u32[]{:S(2)}, u32[]{:S(2)}) collective-permute-start(f32[1,8,32,1024]{3,2,1,0:T(8,128)} %bitcast.250), channel_id=1, source_target_pairs={{0,16},{1,17},{2,18},{3,19},{4,20},{5,21},{6,22},{7,23},{8,24},{9,... | collective-permute-start | bytes 3145736 | tf_op jit(solution)/shard_map/ppermute | solution.py:20
  156.1 6.1 %collective-permute-start.10 = (f32[2,8,1,1024]{3,2,1,0:T(1,128)S(1)}, f32[2,8,1,1024]{3,2,1,0:T(1,128)S(1)}, u32[]{:S(2)}, u32[]{:S(2)}) collective-permute-start(f32[2,8,1,1024]{3,2,1,0:T(1,128)S(1)} %get-tuple-element.301), channel_id=1, source_target_pairs={{1,0},{2,1},{3,2},{4,3},{5,4},{6,5},{7,6},{8,7},{9,8},{10,9},{11,1... | collective-permute-start | bytes 196616 | tf_op jit(solution)/shard_map/ppermute | solution.py:22
  160.1 6.8 %collective-permute-start.11 = (f32[2,8,1,1024]{3,2,1,0:T(1,128)S(1)}, f32[2,8,1,1024]{3,2,1,0:T(1,128)S(1)}, u32[]{:S(2)}, u32[]{:S(2)}) collective-permute-start(f32[2,8,1,1024]{3,2,1,0:T(1,128)S(1)} %get-tuple-element.302), channel_id=1, source_target_pairs={{0,1},{1,2},{2,3},{3,4},{4,5},{5,6},{6,7},{7,8},{8,9},{9,10},{10,1... | collective-permute-start | bytes 196616 | tf_op jit(solution)/shard_map/ppermute | solution.py:20
  169.4 5.7 %collective-permute-start.12 = (f32[2,8,1,1024]{3,2,1,0:T(1,128)S(1)}, f32[2,8,1,1024]{3,2,1,0:T(1,128)S(1)}, u32[]{:S(2)}, u32[]{:S(2)}) collective-permute-start(f32[2,8,1,1024]{3,2,1,0:T(1,128)S(1)} %get-tuple-element.295), channel_id=1, source_target_pairs={{1,0},{2,1},{3,2},{4,3},{5,4},{6,5},{7,6},{8,7},{9,8},{10,9},{11,1... | collective-permute-start | bytes 196616 | tf_op jit(solution)/shard_map/ppermute | solution.py:22
  171.3 6.9 %collective-permute-start.13 = (f32[2,8,1,1024]{3,2,1,0:T(1,128)S(1)}, f32[2,8,1,1024]{3,2,1,0:T(1,128)S(1)}, u32[]{:S(2)}, u32[]{:S(2)}) collective-permute-start(f32[2,8,1,1024]{3,2,1,0:T(1,128)S(1)} %get-tuple-element.296), channel_id=1, source_target_pairs={{0,1},{1,2},{2,3},{3,4},{4,5},{5,6},{6,7},{7,8},{8,9},{9,10},{10,1... | collective-permute-start | bytes 196616 | tf_op jit(solution)/shard_map/ppermute | solution.py:20
  178.2 1.6 copy-start.5
  179.8 9.4 %copy-start.7 = (f32[8,32,1024]{2,1,0:T(8,128)S(1)}, f32[8,32,1024]{2,1,0:T(8,128)}, u32[]{:S(2)}) copy-start(f32[8,32,1024]{2,1,0:T(8,128)} %get-tuple-element.286) | copy-start | bytes 3145732
  179.8 9.4 %copy-start.11 = (f32[1,8,32,1024]{3,2,1,0:T(8,128)S(1)}, f32[1,8,32,1024]{3,2,1,0:T(8,128)}, u32[]{:S(2)}) copy-start(f32[1,8,32,1024]{3,2,1,0:T(8,128)} %param.25) | copy-start | bytes 3145732
  179.8 9.4 %copy-start.12 = (f32[1,8,32,1024]{3,2,1,0:T(8,128)S(1)}, f32[1,8,32,1024]{3,2,1,0:T(8,128)}, u32[]{:S(2)}) copy-start(f32[1,8,32,1024]{3,2,1,0:T(8,128)} %param.24) | copy-start | bytes 3145732
  180.3 8.9 %collective-permute-start.14 = (f32[8,32,1024]{2,1,0:T(8,128)S(1)}, f32[8,32,1024]{2,1,0:T(8,128)S(1)}, u32[]{:S(2)}, u32[]{:S(2)}) collective-permute-start(f32[8,32,1024]{2,1,0:T(8,128)S(1)} %bitcast_multiply_fusion.5), channel_id=1, source_target_pairs={{16,0},{17,1},{18,2},{19,3},{20,4},{21,5},{22,6},{23,7},{24,8},{25... | collective-permute-start | bytes 3145736 | tf_op jit(solution)/shard_map/ppermute | solution.py:32
  191.2 6.1 %copy-start.1 = (s32[1,16,128]{2,1,0:T(8,128)S(1)}, s32[1,16,128]{2,1,0:T(8,128)}, u32[]{:S(2)}) copy-start(s32[1,16,128]{2,1,0:T(8,128)} %param.30) | copy-start | bytes 24580
  191.2 4.7 %collective-permute-start.15 = (f32[8,32,1024]{2,1,0:T(8,128)S(1)}, f32[8,32,1024]{2,1,0:T(8,128)S(1)}, u32[]{:S(2)}, u32[]{:S(2)}) collective-permute-start(f32[8,32,1024]{2,1,0:T(8,128)S(1)} %get-tuple-element.287), channel_id=1, source_target_pairs={{0,16},{1,17},{2,18},{3,19},{4,20},{5,21},{6,22},{7,23},{8,24},{9,... | collective-permute-start | bytes 3145736 | tf_op jit(solution)/shard_map/ppermute | solution.py:32
where the time goes:
time: 198 us; the launch traced here: 197 us
  starting transfers between devices  77 us (39%)
  waiting for transfers between devices  34.7 us (18%)
  matrix products  32.8 us (17%)
  other arithmetic  30.4 us (15%)
  local copies, waits for them, and re-layouts  20.5 us (10%)
    ppermute x6, starting transfers between devices, with_halo(): lax.ppermute(head, axis, [((i + 1) % count, i) for i in range(ends)])  23.8 us
    ppermute x6, waiting for transfers between devices, with_halo(): lax.ppermute(tail, axis, [(i, (i + 1) % count) for i in range(ends)])  15.6 us
    ppermute x4, starting transfers between devices, shifted(): return lax.ppermute(value, axis, pairs)  15.1 us
    ppermute x6, starting transfers between devices, with_halo(): lax.ppermute(tail, axis, [(i, (i + 1) % count) for i in range(ends)])  13.6 us
    all_to_all x2, starting transfers between devices, on_device(): lax.all_to_all(sent_grad, 'space', split_axis=0, concat_axis=0, tiled=True)  9.85 us
    all_to_all x2, starting transfers between devices, on_device(): lax.all_to_all(wanted, 'space', split_axis=0, concat_axis=0, tiled=True)  7.98 us
    sub x2, other arithmetic, on_device(): source = r_model - err_field * upward  7.46 us
    dot_general x8, matrix products, spread_per_block(): jnp.einsum('sr,slc->lrc', row_onehot, lines, precision=lax.Precision.HIGH...  7.22 us
  transfers between devices with their start and end apart: 21, of which 11 were waited for; matrix products, arithmetic and copies ran while one was open for 20% of the time, Pallas kernels for 0%

commit v1 on v0

v1 whole, which is shorter than its diff:
```python
import functools

import jax
import jax.numpy as jnp
from jax import lax
from jax.experimental import pallas as pl
from jax.experimental.pallas import tpu as pltpu
from jax.sharding import PartitionSpec as P

SUBSTEPS = 2
ITERS = 2
EDGE = 8
F32 = jnp.float32
BF16 = jnp.bfloat16
MESH = pl.DeviceIdType.MESH
LOADS = ("inc", "dual", "rhs", "err", "dec", "scale", "field", "jac")


def contract(a, b, dims):
    return lax.dot_general(a, b, (dims, ((), ())), preferred_element_type=F32)


def kernel(
    n, cap,
    inc_in, dual_in, dobs_in, rhs_in, err_in, dec_in, scale_in, diff_ref, owners_ref,
    cols_ref, jac_in, innov_ref, ovar_ref,
    dual_out, dobs_out, inc_out,
    inc, dual, rhs, err, dec, scale, field, jac,
    adj, mfield, perm, perm_t, pick, pick_t, lines, packed, vmat, image, obs_dual,
    req_s, req_r, col_lo, col_hi, msg_s, msg_r, halo_s, halo_r, pair_s, pair_r,
    load_sem, out_sem, a2a_send, a2a_recv, halo_send, halo_recv, pair_send, pair_recv,
):
    me = lax.axis_index("space")
    tm = lax.axis_index("tm")
    lev, rows, width = inc.shape
    tiles, touched = cols_ref.shape[1:]
    slots = n * cap
    span = cap * lev
    groups = width // 128
    own = pl.ds(EDGE, rows)

    def load(k, src, dst):
        return pltpu.make_async_copy(src, dst, load_sem.at[LOADS.index(k)])

    loads = {
        "inc": load("inc", inc_in.at[0], inc),
        "dual": load("dual", dual_in.at[0], dual),
        "rhs": load("rhs", rhs_in.at[0], rhs),
        "err": load("err", err_in.at[0], err),
        "dec": load("dec", dec_in.at[0], dec),
        "scale": load("scale", scale_in, scale.at[:, own]),
        "jac": load("jac", jac_in.at[0], jac),
    }
    field_0 = load("field", inc_in.at[0], field.at[:, own])
    field_1 = load("field", dual_in.at[0], field.at[:, own])

    @pl.when(tm == 0)
    def _():
        field_0.start()

    @pl.when(tm == 1)
    def _():
        field_1.start()

    for name in ("scale", "jac", "inc", "dual", "dec", "rhs", "err"):
        loads[name].start()

    barrier = pltpu.get_barrier_semaphore()

    def greet(k, c):
        pl.semaphore_signal(
            barrier, inc=1, device_id={"space": lax.rem(me + k, n)}, device_id_type=MESH
        )
        return c

    lax.fori_loop(1, n, greet, 0)
    pl.semaphore_signal(barrier, inc=1, device_id={"tm": 1 - tm}, device_id_type=MESH)

    zero_rows = jnp.zeros((EDGE, width), F32)
    for l in range(lev):
        for ref in (field, scale):
            ref[l, pl.ds(0, EDGE), :] = zero_rows
            ref[l, pl.ds(EDGE + rows, EDGE), :] = zero_rows

    owner = [owners_ref[0, t] for t in range(tiles)]
    slot_of = []
    for t in range(tiles):
        rank = jnp.int32(0)
        for u in range(t):
            rank = rank + jnp.where(owner[u] == owner[t], 1, 0)
        slot_of.append(owner[t] * cap + rank)
    slot_row = lax.broadcasted_iota(jnp.int32, (slots, touched), 0)
    wide_row = lax.broadcasted_iota(jnp.int32, (slots * lev, touched), 0) // lev

    wanted = jnp.zeros((slots * lev, touched), jnp.int32)
    for t in range(tiles):
        wanted = jnp.where(wide_row == slot_of[t], cols_ref[0, pl.ds(t, 1), :], wanted)
    req_s[...] = wanted

    def block(i):
        return pl.ds(pl.multiple_of(i * span, span), span)

    def phase_refs(phase):
        if phase == 0:
            return req_s, req_r
        return msg_s.at[phase - 1], msg_r.at[phase - 1]

    def exchange(phase, to):
        src, dst = phase_refs(phase)
        return pltpu.make_async_remote_copy(
            src_ref=src.at[block(to)],
            dst_ref=dst.at[block(me)],
            send_sem=a2a_send.at[phase, to],
            recv_sem=a2a_recv.at[phase, me],
            device_id={"space": to},
            device_id_type=MESH,
        )

    def arrival(phase, frm):
        src, dst = phase_refs(phase)
        return pltpu.make_async_remote_copy(
            src_ref=src.at[block(frm)],
            dst_ref=dst.at[block(frm)],
            send_sem=a2a_send.at[phase, frm],
            recv_sem=a2a_recv.at[phase, frm],
            device_id={"space": frm},
            device_id_type=MESH,
        )

    def over_peers(act):
        def step(k, c):
            act(lax.rem(me + k, n))
            return c

        lax.fori_loop(1, n, step, 0)

    def send_all(phase):
        over_peers(lambda to: exchange(phase, to).start())
        src, dst = phase_refs(phase)
        dst[block(me), :] = src[block(me), :]

    def recv_all(phase):
        over_peers(lambda frm: arrival(phase, frm).wait_recv())

    pl.semaphore_wait(barrier, n)
    send_all(0)

    def halo_copy(it, way):
        count = 4 * lev if it == 0 else 2 * lev
        part = pl.ds(0, count)
        return pltpu.make_async_remote_copy(
            src_ref=halo_s.at[it, way, part],
            dst_ref=halo_r.at[it, way, part],
            send_sem=halo_send.at[it, way],
            recv_sem=halo_recv.at[it, way],
            device_id={"space": lax.rem(me + (n - 1 if way == 0 else 1), n)},
            device_id_type=MESH,
        )

    def halo_out(it):
        for way, first in ((0, EDGE), (1, EDGE + rows - 2)):
            for l in range(lev):
                halo_s[it, way, pl.ds(2 * l, 2), :] = field[l, pl.ds(first, 2), :]
                if it == 0:
                    halo_s[it, way, pl.ds(2 * (lev + l), 2), :] = scale[l, pl.ds(first, 2), :]

        @pl.when(me > 0)
        def _():
            halo_copy(it, 0).start()

        @pl.when(me < n - 1)
        def _():
            halo_copy(it, 1).start()

    def halo_in(it):
        def place(way, first):
            halo_copy(it, way).wait_recv()
            for l in range(lev):
                field[l, pl.ds(first, 2), :] = halo_r[it, way, pl.ds(2 * l, 2), :]
                if it == 0:
                    scale[l, pl.ds(first, 2), :] = halo_r[it, way, pl.ds(2 * (lev + l), 2), :]

        @pl.when(me < n - 1)
        def _():
            place(0, EDGE + rows)

        @pl.when(me > 0)
        def _():
            place(1, EDGE - 2)

    def pair_copy(it, kind, l):
        return pltpu.make_async_remote_copy(
            src_ref=pair_s.at[it, kind, l],
            dst_ref=pair_r.at[it, kind, l],
            send_sem=pair_send.at[it, kind, l],
            recv_sem=pair_recv.at[it, kind, l],
            device_id={"tm": 1 - tm},
            device_id_type=MESH,
        )

    def per_level(act):
        def step(l, c):
            act(l)
            return c

        lax.fori_loop(0, lev, step, 0)

    def model(l):
        factor = scale[l]
        current = field[l]
        tall = current.shape[0]
        for repeat in range(SUBSTEPS):
            scaled = factor * current
            laplace = (
                pltpu.roll(scaled, 1, 0)
                + pltpu.roll(scaled, tall - 1, 0)
                + pltpu.roll(scaled, 1, 1)
                + pltpu.roll(scaled, width - 1, 1)
                - 4.0 * scaled
            )
            current = factor * (scaled + diff_ref[l] * laplace)
        return current[EDGE : EDGE + rows]

    def adjoint_out(phase):
        rounded = obs_dual[...].astype(BF16).astype(F32)
        for t in range(tiles):
            row = jnp.where(slot_row == slot_of[t], rounded[t : t + 1, :], 0.0)
            vmat[:, pl.ds(t * touched, touched)] = row.astype(BF16)
        flat = jac[...].reshape(tiles * jac.shape[1], jac.shape[2])
        grad = contract(vmat[...], flat, ((1,), (0,))).astype(BF16)
        grad = contract(grad, perm_t[...], ((1,), (0,)))
        for l in range(lev):
            packed[pl.ds(l, slots, stride=lev), :] = grad[:, l * touched : (l + 1) * touched]
        phase_refs(phase)[0][...] = packed[...].astype(BF16)
        send_all(phase)

    def columns_out(phase):
        flat = inc[...].reshape(lev * rows, width).astype(BF16)
        lines[...] = contract(pick[...], flat, ((1,), (0,)))
        found = jnp.zeros((slots * lev, touched), F32)
        for h in range(groups):
            part = jnp.take_along_axis(
                lines[:, h * 128 : (h + 1) * 128], col_lo[...], axis=1, mode="promise_in_bounds"
            )
            found = jnp.where(col_hi[...] == h, part, found)
        phase_refs(phase)[0][...] = found.astype(BF16)
        send_all(phase)

    def observe(phase):
        recv_all(phase)
        packed[...] = phase_refs(phase)[1][...].astype(F32)
        cells = jnp.concatenate(
            [packed[pl.ds(l, slots, stride=lev), :] for l in range(lev)], axis=1
        ).astype(BF16)
        cells = contract(cells, perm[...], ((1,), (0,))).astype(BF16)
        flat = jac[...].reshape(tiles * jac.shape[1], jac.shape[2])
        seen = contract(cells, flat, ((1,), (1,)))
        for t in range(tiles):
            mine = jnp.where(slot_row == slot_of[t], seen[:, t * touched : (t + 1) * touched], 0.0)
            image[pl.ds(t, 1), :] = jnp.sum(mine, axis=0, keepdims=True)
        variance = ovar_ref[0].astype(F32)
        held = obs_dual[...]
        residual = innov_ref[0].astype(F32) - variance * held - image[...]
        obs_dual[...] = held + residual / variance

    def spread(phase):
        recv_all(phase)
        packed[...] = phase_refs(phase)[1][...].astype(F32)
        lane_row = lax.broadcasted_iota(jnp.int32, (128, touched), 0)

        def slot_lines(s, c):
            here = pl.ds(pl.multiple_of(s * lev, lev), lev)
            values, high, low = packed[here, :], col_hi[here, :], col_lo[here, :]
            left = jnp.concatenate(
                [jnp.where(high == h, values, 0.0) for h in range(groups)], axis=0
            ).astype(BF16)
            places = jnp.concatenate([low] * (128 // lev), axis=0)
            onehot = jnp.where(places == lane_row, 1.0, 0.0).astype(BF16)
            line = contract(left, onehot, ((1,), (1,)))
            for h in range(groups):
                lines[here, pl.ds(h * 128, 128)] = line[h * lev : (h + 1) * lev]
            return c

        def four(s, c):
            for u in range(4):
                slot_lines(4 * s + u, c)
            return c

        lax.fori_loop(0, slots // 4, four, 0)
        whole = lines[...]
        high = whole.astype(BF16)
        low = (whole - high.astype(F32)).astype(BF16)
        total = contract(pick_t[...], high, ((1,), (0,))) + contract(
            pick_t[...], low, ((1,), (0,))
        )
        adj[...] = total.reshape(lev, rows, width)

    loads["scale"].wait()
    field_0.wait()
    halo_out(0)

    cells_all = touched * lev
    first = lax.broadcasted_iota(jnp.int32, (cells_all, cells_all), 0)
    second = lax.broadcasted_iota(jnp.int32, (cells_all, cells_all), 1)
    perm_t[...] = jnp.where((first % lev) * touched + first // lev == second, 1.0, 0.0).astype(BF16)
    perm[...] = jnp.where((first % touched) * lev + first // touched == second, 1.0, 0.0).astype(
        BF16
    )
    obs_dual[...] = dobs_in[0].astype(F32)
    loads["jac"].wait()
    adjoint_out(1)

    recv_all(0)
    cell = req_r[...]
    column = cell % width
    col_lo[...] = column % 128
    col_hi[...] = column // 128
    line_of = cell // width
    level_of = lax.broadcasted_iota(jnp.int32, (slots * lev, touched), 0) % lev
    place = level_of * rows + line_of
    lane = lax.broadcasted_iota(jnp.int32, (slots * lev, touched), 1)
    chosen = jnp.concatenate(
        [
            jnp.where(place == lane + first_lane, 1.0, 0.0)
            for first_lane in range(0, lev * rows, touched)
        ],
        axis=1,
    )
    pick[...] = chosen.astype(BF16)
    pick_t[...] = chosen.T.astype(BF16)

    loads["inc"].wait()
    columns_out(2)
    loads["dual"].wait()
    loads["dec"].wait()
    loads["rhs"].wait()
    loads["err"].wait()

    for it in range(ITERS):
        last = it == ITERS - 1
        grad_phase, cols_phase = 1 + 2 * it, 2 + 2 * it
        halo_in(it)

        @pl.when(tm == 0)
        def _():
            def go(l):
                pair_s[it, 0, l] = model(l)
                pair_copy(it, 0, l).start()

            per_level(go)

        @pl.when(tm == 1)
        def _():
            def go(l):
                mfield[l] = model(l)

            per_level(go)

        spread(grad_phase)

        @pl.when(tm == 1)
        def _():
            def go(l):
                upward = -dual[l] - adj[l]
                pair_s[it, 2, l] = mfield[l] + dec[l] * upward
                pair_copy(it, 2, l).start()
                r_model = rhs[l] - err[l] * dual[l] - inc[l]
                mfield[l] = r_model - err[l] * upward
                raised = dual[l] + upward
                dual[l] = raised
                if not last:
                    field[l, own, :] = raised
                else:
                    pltpu.make_async_copy(dual.at[l], dual_out.at[0, l], out_sem.at[0, l]).start()

            per_level(go)

        if not last:
            observe(cols_phase)
            adjoint_out(grad_phase + 2)

        @pl.when(tm == 0)
        def _():
            def go(l):
                pair_copy(it, 2, l).wait_recv()
                upward = pair_r[it, 2, l] - dual[l] - adj[l]
                along = rhs[l] - err[l] * dual[l] - inc[l] - err[l] * upward
                pair_s[it, 1, l] = along
                pair_copy(it, 1, l).start()
                dual[l] = dual[l] + upward
                moved = inc[l] + along
                inc[l] = moved
                if not last:
                    field[l, own, :] = moved
                else:
                    pltpu.make_async_copy(dual.at[l], dual_out.at[0, l], out_sem.at[0, l]).start()
                    pltpu.make_async_copy(inc.at[l], inc_out.at[0, l], out_sem.at[1, l]).start()

            per_level(go)

        if not last:
            halo_out(it + 1)
        else:
            observe(cols_phase)
            dobs_out[0] = obs_dual[...]

        @pl.when(tm == 1)
        def _():
            def go(l):
                pair_copy(it, 0, l).wait_recv()
                pair_copy(it, 1, l).wait_recv()
                along = mfield[l] + pair_r[it, 0, l] + dec[l] * pair_r[it, 1, l]
                inc[l] = inc[l] + along
                if last:
                    pltpu.make_async_copy(inc.at[l], inc_out.at[0, l], out_sem.at[1, l]).start()

            per_level(go)

        if not last:
            columns_out(cols_phase + 2)

    for phase in range(1 + 2 * ITERS):
        over_peers(lambda to: exchange(phase, to).wait_send())
    for it in range(ITERS):

        @pl.when(me > 0)
        def _():
            halo_copy(it, 0).wait_send()

        @pl.when(me < n - 1)
        def _():
            halo_copy(it, 1).wait_send()

        @pl.when(tm == 0)
        def _():
            per_level(lambda l: pair_copy(it, 0, l).wait_send())
            per_level(lambda l: pair_copy(it, 1, l).wait_send())

        @pl.when(tm == 1)
        def _():
            per_level(lambda l: pair_copy(it, 2, l).wait_send())

    per_level(lambda l: pltpu.make_async_copy(dual.at[l], dual_out.at[0, l], out_sem.at[0, l]).wait())
    per_level(lambda l: pltpu.make_async_copy(inc.at[l], inc_out.at[0, l], out_sem.at[1, l]).wait())


def on_device(*args):
    increment_start, jacobian, tile_cols = args[0], args[10], args[9]
    lev, rows, width = increment_start.shape[1:]
    tiles, touched = tile_cols.shape[1:]
    orows = jacobian.shape[2]
    n = lax.axis_size("space")
    cap = max(2, 2 * tiles // n)
    slots = n * cap
    cells = touched * lev
    grid = (lev, rows, width)
    tall = (lev, rows + 2 * EDGE, width)
    hbm = pl.BlockSpec(memory_space=pl.ANY)
    vmem = pl.BlockSpec(memory_space=pltpu.VMEM)
    smem = pl.BlockSpec(memory_space=pltpu.SMEM)
    dma = pltpu.SemaphoreType.DMA
    scratch = [
        pltpu.VMEM(grid, F32),
        pltpu.VMEM(grid, F32),
        pltpu.VMEM(grid, F32),
        pltpu.VMEM(grid, F32),
        pltpu.VMEM(grid, F32),
        pltpu.VMEM(tall, F32),
        pltpu.VMEM(tall, F32),
        pltpu.VMEM((tiles, orows, cells), BF16),
        pltpu.VMEM(grid, F32),
        pltpu.VMEM(grid, F32),
        pltpu.VMEM((cells, cells), BF16),
        pltpu.VMEM((cells, cells), BF16),
        pltpu.VMEM((slots * lev, lev * rows), BF16),
        pltpu.VMEM((lev * rows, slots * lev), BF16),
        pltpu.VMEM((slots * lev, width), F32),
        pltpu.VMEM((slots * lev, touched), F32),
        pltpu.VMEM((slots, tiles * orows), BF16),
        pltpu.VMEM((tiles, orows), F32),
        pltpu.VMEM((tiles, orows), F32),
        pltpu.VMEM((slots * lev, touched), jnp.int32),
        pltpu.VMEM((slots * lev, touched), jnp.int32),
        pltpu.VMEM((slots * lev, touched), jnp.int32),
        pltpu.VMEM((slots * lev, touched), jnp.int32),
        pltpu.VMEM((2 * ITERS, slots * lev, touched), BF16),
        pltpu.VMEM((2 * ITERS, slots * lev, touched), BF16),
        pltpu.VMEM((ITERS, 2, 4 * lev, width), F32),
        pltpu.VMEM((ITERS, 2, 4 * lev, width), F32),
        pltpu.VMEM((ITERS, 3) + grid, F32),
        pltpu.VMEM((ITERS, 3) + grid, F32),
        dma((len(LOADS),)),
        dma((2, lev)),
        dma((1 + 2 * ITERS, n)),
        dma((1 + 2 * ITERS, n)),
        dma((ITERS, 2)),
        dma((ITERS, 2)),
        dma((ITERS, 3, lev)),
        dma((ITERS, 3, lev)),
    ]
    return pl.pallas_call(
        functools.partial(kernel, n, cap),
        out_shape=(
            jax.ShapeDtypeStruct((1,) + grid, F32),
            jax.ShapeDtypeStruct((1, tiles, orows), F32),
            jax.ShapeDtypeStruct((1,) + grid, F32),
        ),
        in_specs=[hbm, hbm, vmem, hbm, hbm, hbm, hbm, smem, smem, vmem, hbm, vmem, vmem],
        out_specs=(hbm, vmem, hbm),
        scratch_shapes=scratch,
        compiler_params=pltpu.CompilerParams(
            collective_id=0, has_side_effects=True, vmem_limit_bytes=60 * 2**20
        ),
        name="assimilate",
    )(*args)


def solution(mesh):
    in_specs = (
        P("tm", None, "space", None),
        P("tm", None, "space", None),
        P("tm", "space", None),
        P("tm", None, "space", None),
        P("tm", None, "space", None),
        P("tm", None, "space", None),
        P(None, "space", None),
        P(),
        P("tm", "space"),
        P("tm", "space", None),
        P("tm", "space", None, None),
        P("tm", "space", None),
        P("tm", "space", None),
    )
    out_specs = (P("tm", None, "space", None), P("tm", "space", None), P("tm", None, "space", None))
    return jax.shard_map(
        on_device, mesh=mesh, in_specs=in_specs, out_specs=out_specs, check_vma=False
    )
```

time: 198 us -> 48 us (0.24)
  the two profiles are of different devices: /device:TPU:9 before, /device:TPU:0 now
where the time goes in v1:
time: 48 us; the launch traced here: 47.7 us
  Pallas kernels  41.2 us (86%)
  local copies, waits for them, and re-layouts  5.91 us (12%)
  between operations  0.64 us (1%)
    pallas_call x1, Pallas kernels, on_device(): pl.pallas_call(functools.partial(kernel, n, cap), out_shape=(jax.ShapeDty...  41.2 us
    unnamed x3, local copies, waits for them, and re-layouts  5.91 us

profile of v1, /device:TPU:0, one launch (start us, length us, event | category | flops | bytes accessed | tf_op | source)
XLA Modules:
  0.0 47.7 jit_solution(16617913818850452956)
XLA Ops:
  0.6 41.2 %assimilate.1 = (f32[1,8,32,1024]{3,2,1,0:T(8,128)}, f32[1,16,128]{2,1,0:T(8,128)}, f32[1,8,32,1024]{3,2,1,0:T(8,128)}) custom-call(f32[1,8,32,1024]{3,2,1,0:T(8,128)} %inc_in.1, f32[1,8,32,1024]{3,2,1,0:T(8,128)} %dual_in.1, bf16[1,16,128]{2,1,0:T(8,128)(2,1)} %dobs_in.1, f32[1,8,32,1024]{3,2,1,0:T(8,128)} %rhs_in.1, f32[1,8,32,1024]{3,2,1,0:T(8,128)} %err_in.1, ...), custom_call_target="tpu_custom_call" | custom-call | tf_op jit(solution)/shard_map/assimilate/pallas_call | solution.py:501
  41.8 2.3 %copy.19 = f32[1,8,32,1024]{3,2,1,0:T(8,128)} copy(f32[1,8,32,1024]{3,2,1,0:T(8,128)} %get-tuple-element.6) | data formatting | bytes 2097152
  44.1 1.3 %copy.20 = f32[1,16,128]{2,1,0:T(8,128)} copy(f32[1,16,128]{2,1,0:T(8,128)} %get-tuple-element.7) | data formatting | bytes 16384
  45.4 2.3 %copy.21 = f32[1,8,32,1024]{3,2,1,0:T(8,128)} copy(f32[1,8,32,1024]{3,2,1,0:T(8,128)} %get-tuple-element.8) | data formatting | bytes 2097152

commit v2 on v1

--- a/solution.py
+++ b/solution.py
@@ -16,6 +16,20 @@
 LOADS = ("inc", "dual", "rhs", "err", "dec", "scale", "field", "jac")
 
 
+def shift_of(size):
+    assert size & (size - 1) == 0
+    return size.bit_length() - 1
+
+
+def reorder(cells, parts, dtype):
+    row = lax.broadcasted_iota(jnp.int32, (cells, 128), 0)
+    lane = lax.broadcasted_iota(jnp.int32, (cells, 128), 1)
+    target = (row & (parts - 1)) * (cells // parts) + (row >> shift_of(parts)) - lane
+    return jnp.concatenate(
+        [jnp.where(target == at, 1.0, 0.0).astype(dtype) for at in range(0, cells, 128)], axis=1
+    )
+
+
 def contract(a, b, dims):
     return lax.dot_general(a, b, (dims, ((), ())), preferred_element_type=F32)
 
@@ -26,7 +40,7 @@
     cols_ref, jac_in, innov_ref, ovar_ref,
     dual_out, dobs_out, inc_out,
     inc, dual, rhs, err, dec, scale, field, jac,
-    adj, mfield, perm, perm_t, pick, pick_t, lines, packed, vmat, image, obs_dual,
+    adj, mfield, source, perm, perm_t, pick, pick_t, lines, packed, vmat, image, obs_dual,
     req_s, req_r, col_lo, col_hi, msg_s, msg_r, halo_s, halo_r, pair_s, pair_r,
     load_sem, out_sem, a2a_send, a2a_recv, halo_send, halo_recv, pair_send, pair_recv,
 ):
@@ -90,7 +104,7 @@
             rank = rank + jnp.where(owner[u] == owner[t], 1, 0)
         slot_of.append(owner[t] * cap + rank)
     slot_row = lax.broadcasted_iota(jnp.int32, (slots, touched), 0)
-    wide_row = lax.broadcasted_iota(jnp.int32, (slots * lev, touched), 0) // lev
+    wide_row = lax.broadcasted_iota(jnp.int32, (slots * lev, touched), 0) >> shift_of(lev)
 
     wanted = jnp.zeros((slots * lev, touched), jnp.int32)
     for t in range(tiles):
@@ -281,12 +295,12 @@
                 lines[here, pl.ds(h * 128, 128)] = line[h * lev : (h + 1) * lev]
             return c
 
-        def four(s, c):
-            for u in range(4):
-                slot_lines(4 * s + u, c)
+        def eight(s, c):
+            for u in range(8):
+                slot_lines(8 * s + u, c)
             return c
 
-        lax.fori_loop(0, slots // 4, four, 0)
+        lax.fori_loop(0, slots // 8, eight, 0)
         whole = lines[...]
         high = whole.astype(BF16)
         low = (whole - high.astype(F32)).astype(BF16)
@@ -300,23 +314,18 @@
     halo_out(0)
 
     cells_all = touched * lev
-    first = lax.broadcasted_iota(jnp.int32, (cells_all, cells_all), 0)
-    second = lax.broadcasted_iota(jnp.int32, (cells_all, cells_all), 1)
-    perm_t[...] = jnp.where((first % lev) * touched + first // lev == second, 1.0, 0.0).astype(BF16)
-    perm[...] = jnp.where((first % touched) * lev + first // touched == second, 1.0, 0.0).astype(
-        BF16
-    )
+    perm_t[...] = reorder(cells_all, lev, BF16)
+    perm[...] = reorder(cells_all, touched, BF16)
     obs_dual[...] = dobs_in[0].astype(F32)
     loads["jac"].wait()
     adjoint_out(1)
 
     recv_all(0)
     cell = req_r[...]
-    column = cell % width
-    col_lo[...] = column % 128
-    col_hi[...] = column // 128
-    line_of = cell // width
-    level_of = lax.broadcasted_iota(jnp.int32, (slots * lev, touched), 0) % lev
+    col_lo[...] = cell & 127
+    col_hi[...] = (cell & (width - 1)) >> 7
+    line_of = cell >> shift_of(width)
+    level_of = lax.broadcasted_iota(jnp.int32, (slots * lev, touched), 0) & (lev - 1)
     place = level_of * rows + line_of
     lane = lax.broadcasted_iota(jnp.int32, (slots * lev, touched), 1)
     chosen = jnp.concatenate(
@@ -336,25 +345,39 @@
     loads["rhs"].wait()
     loads["err"].wait()
 
+    def forward_model(it):
+        halo_in(it)
+
+        def go(l):
+            pair_s[it, 0, l] = model(l)
+            pair_copy(it, 0, l).start()
+
+        per_level(go)
+
+    def backward_model(it):
+        halo_in(it)
+
+        def go(l):
+            mfield[l] = model(l)
+
+        per_level(go)
+
+    def write_out(l, which):
+        held, out = ((dual, dual_out), (inc, inc_out))[which]
+        return pltpu.make_async_copy(held.at[l], out.at[0, l], out_sem.at[which, l])
+
     for it in range(ITERS):
         last = it == ITERS - 1
         grad_phase, cols_phase = 1 + 2 * it, 2 + 2 * it
-        halo_in(it)
-
-        @pl.when(tm == 0)
-        def _():
-            def go(l):
-                pair_s[it, 0, l] = model(l)
-                pair_copy(it, 0, l).start()
-
-            per_level(go)
-
-        @pl.when(tm == 1)
-        def _():
-            def go(l):
-                mfield[l] = model(l)
-
-            per_level(go)
+        if it == 0:
+
+            @pl.when(tm == 0)
+            def _():
+                forward_model(it)
+
+            @pl.when(tm == 1)
+            def _():
+                backward_model(it)
 
         spread(grad_phase)
 
@@ -365,15 +388,17 @@
                 pair_s[it, 2, l] = mfield[l] + dec[l] * upward
                 pair_copy(it, 2, l).start()
                 r_model = rhs[l] - err[l] * dual[l] - inc[l]
-                mfield[l] = r_model - err[l] * upward
+                source[l] = r_model - err[l] * upward
                 raised = dual[l] + upward
                 dual[l] = raised
                 if not last:
                     field[l, own, :] = raised
                 else:
-                    pltpu.make_async_copy(dual.at[l], dual_out.at[0, l], out_sem.at[0, l]).start()
+                    write_out(l, 0).start()
 
             per_level(go)
+            if not last:
+                halo_out(it + 1)
 
         if not last:
             observe(cols_phase)
@@ -381,6 +406,9 @@
 
         @pl.when(tm == 0)
         def _():
+            if it > 0:
+                forward_model(it)
+
             def go(l):
                 pair_copy(it, 2, l).wait_recv()
                 upward = pair_r[it, 2, l] - dual[l] - adj[l]
@@ -393,26 +421,29 @@
                 if not last:
                     field[l, own, :] = moved
                 else:
-                    pltpu.make_async_copy(dual.at[l], dual_out.at[0, l], out_sem.at[0, l]).start()
-                    pltpu.make_async_copy(inc.at[l], inc_out.at[0, l], out_sem.at[1, l]).start()
+                    write_out(l, 0).start()
+                    write_out(l, 1).start()
 
             per_level(go)
-
-        if not last:
-            halo_out(it + 1)
-        else:
+            if not last:
+                halo_out(it + 1)
+
+        if last:
             observe(cols_phase)
             dobs_out[0] = obs_dual[...]
 
         @pl.when(tm == 1)
         def _():
+            if not last:
+                backward_model(it + 1)
+
             def go(l):
                 pair_copy(it, 0, l).wait_recv()
                 pair_copy(it, 1, l).wait_recv()
-                along = mfield[l] + pair_r[it, 0, l] + dec[l] * pair_r[it, 1, l]
+                along = source[l] + pair_r[it, 0, l] + dec[l] * pair_r[it, 1, l]
                 inc[l] = inc[l] + along
                 if last:
-                    pltpu.make_async_copy(inc.at[l], inc_out.at[0, l], out_sem.at[1, l]).start()
+                    write_out(l, 1).start()
 
             per_level(go)
 
@@ -440,8 +471,26 @@
         def _():
             per_level(lambda l: pair_copy(it, 2, l).wait_send())
 
-    per_level(lambda l: pltpu.make_async_copy(dual.at[l], dual_out.at[0, l], out_sem.at[0, l]).wait())
-    per_level(lambda l: pltpu.make_async_copy(inc.at[l], inc_out.at[0, l], out_sem.at[1, l]).wait())
+    per_level(lambda l: write_out(l, 0).wait())
+    per_level(lambda l: write_out(l, 1).wait())
+
+
+def deliver(*refs):
+    count = (len(refs) - 1) // 2
+    sources, targets, sem = refs[:count], refs[count : 2 * count], refs[-1]
+    copies = []
+    for src, dst in zip(sources, targets):
+        for part in range(sem.shape[1]) if src.shape[1] == sem.shape[1] else (None,):
+            here = slice(None) if part is None else pl.ds(part, 1)
+            copies.append(
+                pltpu.make_async_copy(
+                    src.at[:, here], dst.at[:, here], sem.at[len(copies) // sem.shape[1], part or 0]
+                )
+            )
+    for copy in copies:
+        copy.start()
+    for copy in copies:
+        copy.wait()
 
 
 def on_device(*args):
@@ -468,6 +517,7 @@
         pltpu.VMEM(tall, F32),
         pltpu.VMEM(tall, F32),
         pltpu.VMEM((tiles, orows, cells), BF16),
+        pltpu.VMEM(grid, F32),
         pltpu.VMEM(grid, F32),
         pltpu.VMEM(grid, F32),
         pltpu.VMEM((cells, cells), BF16),
@@ -498,7 +548,7 @@
         dma((ITERS, 3, lev)),
         dma((ITERS, 3, lev)),
     ]
-    return pl.pallas_call(
+    dual_model, obs_dual, increment = pl.pallas_call(
         functools.partial(kernel, n, cap),
         out_shape=(
             jax.ShapeDtypeStruct((1,) + grid, F32),
@@ -513,6 +563,17 @@
         ),
         name="assimilate",
     )(*args)
+    results = (dual_model, increment, obs_dual)
+    dual_model, increment, obs_dual = pl.pallas_call(
+        deliver,
+        out_shape=tuple(jax.ShapeDtypeStruct(r.shape, r.dtype) for r in results),
+        in_specs=[hbm] * 3,
+        out_specs=(hbm,) * 3,
+        scratch_shapes=[dma((3, lev))],
+        compiler_params=pltpu.CompilerParams(vmem_limit_bytes=60 * 2**20),
+        name="deliver",
+    )(*results)
+    return (dual_model, obs_dual, increment)
 
 
 def solution(mesh):

time: 48 us -> 105 us (2.19)
  Pallas kernels: 41.2 us -> 104 us
  local copies, waits for them, and re-layouts: 5.91 us -> 0 us
    pallas_call x0 -> x1, Pallas kernels: none -> 65.1 us  [on_device(): pl.pallas_call(deliver, out_shape=tuple((jax.ShapeDtypeStruct(r.shape, r....]
    unnamed x3 -> x0, local copies, waits for them, and re-layouts: 5.91 us -> none
    pallas_call x1, Pallas kernels: 41.2 us -> 38.7 us  [on_device(): pl.pallas_call(functools.partial(kernel, n, cap), out_shape=(jax.ShapeDty...]
where the time goes in v2:
time: 105 us; the launch traced here: 104 us
  Pallas kernels  104 us (99%)
    pallas_call x1, Pallas kernels, on_device(): pl.pallas_call(deliver, out_shape=tuple((jax.ShapeDtypeStruct(r.shape, r....  65.1 us
    pallas_call x1, Pallas kernels, on_device(): pl.pallas_call(functools.partial(kernel, n, cap), out_shape=(jax.ShapeDty...  38.7 us

profile of v2, /device:TPU:0, one launch (start us, length us, event | category | flops | bytes accessed | tf_op | source)
XLA Modules:
  0.0 104.5 jit_solution(14281264973145169086)
XLA Ops:
  0.6 38.7 %assimilate.1 = (f32[1,8,32,1024]{3,2,1,0:T(8,128)}, f32[1,16,128]{2,1,0:T(8,128)}, f32[1,8,32,1024]{3,2,1,0:T(8,128)}) custom-call(f32[1,8,32,1024]{3,2,1,0:T(8,128)} %inc_in.1, f32[1,8,32,1024]{3,2,1,0:T(8,128)} %dual_in.1, bf16[1,16,128]{2,1,0:T(8,128)(2,1)} %dobs_in.1, f32[1,8,32,1024]{3,2,1,0:T(8,128)} %rhs_in.1, f32[1,8,32,1024]{3,2,1,0:T(8,128)} %err_in.1, ...), custom_call_target="tpu_custom_call" | custom-call | tf_op jit(solution)/shard_map/assimilate/pallas_call | solution.py:551
  39.4 65.1 %deliver.1 = (f32[1,8,32,1024]{3,2,1,0:T(8,128)}, f32[1,8,32,1024]{3,2,1,0:T(8,128)}, f32[1,16,128]{2,1,0:T(8,128)}) custom-call(f32[1,8,32,1024]{3,2,1,0:T(8,128)} %get-tuple-element.9.refs_0_, f32[1,8,32,1024]{3,2,1,0:T(8,128)} %get-tuple-element.10.refs_1_, f32[1,16,128]{2,1,0:T(8,128)} %get-tuple-element.11.refs_2_), custom_call_target="tpu_custom_call" | custom-call | tf_op jit(solution)/shard_map/deliver/pallas_call | solution.py:567

commit v3 on v2

--- a/solution.py
+++ b/solution.py
@@ -21,13 +21,35 @@
     return size.bit_length() - 1
 
 
-def reorder(cells, parts, dtype):
-    row = lax.broadcasted_iota(jnp.int32, (cells, 128), 0)
-    lane = lax.broadcasted_iota(jnp.int32, (cells, 128), 1)
-    target = (row & (parts - 1)) * (cells // parts) + (row >> shift_of(parts)) - lane
-    return jnp.concatenate(
-        [jnp.where(target == at, 1.0, 0.0).astype(dtype) for at in range(0, cells, 128)], axis=1
-    )
+def lanes(block, index):
+    return jnp.take_along_axis(block, index, axis=1, mode="promise_in_bounds")
+
+
+def cells_to_levels(values, lev, touched):
+    lane = lax.broadcasted_iota(jnp.int32, (values.shape[0], touched), 1)
+    part = touched // lev
+    found = []
+    for l in range(lev):
+        index = (lane & (part - 1)) * lev + l
+        one = jnp.zeros((values.shape[0], touched), values.dtype)
+        for b in range(lev):
+            block = lanes(values[:, b * touched : (b + 1) * touched], index)
+            one = jnp.where(lane >> shift_of(part) == b, block, one)
+        found.append(one)
+    return found
+
+
+def levels_to_cells(values, lev, touched):
+    lane = lax.broadcasted_iota(jnp.int32, values[0].shape, 1)
+    part = touched // lev
+    found = []
+    for b in range(lev):
+        index = b * part + (lane >> shift_of(lev))
+        one = jnp.zeros(values[0].shape, values[0].dtype)
+        for l in range(lev):
+            one = jnp.where((lane & (lev - 1)) == l, lanes(values[l], index), one)
+        found.append(one)
+    return jnp.concatenate(found, axis=1)
 
 
 def contract(a, b, dims):
@@ -40,7 +62,7 @@
     cols_ref, jac_in, innov_ref, ovar_ref,
     dual_out, dobs_out, inc_out,
     inc, dual, rhs, err, dec, scale, field, jac,
-    adj, mfield, source, perm, perm_t, pick, pick_t, lines, packed, vmat, image, obs_dual,
+    adj, mfield, source, pick, pick_t, lines, packed, vmat, image, obs_dual,
     req_s, req_r, col_lo, col_hi, msg_s, msg_r, halo_s, halo_r, pair_s, pair_r,
     load_sem, out_sem, a2a_send, a2a_recv, halo_send, halo_recv, pair_send, pair_recv,
 ):
@@ -241,10 +263,9 @@
             row = jnp.where(slot_row == slot_of[t], rounded[t : t + 1, :], 0.0)
             vmat[:, pl.ds(t * touched, touched)] = row.astype(BF16)
         flat = jac[...].reshape(tiles * jac.shape[1], jac.shape[2])
-        grad = contract(vmat[...], flat, ((1,), (0,))).astype(BF16)
-        grad = contract(grad, perm_t[...], ((1,), (0,)))
-        for l in range(lev):
-            packed[pl.ds(l, slots, stride=lev), :] = grad[:, l * touched : (l + 1) * touched]
+        grad = contract(vmat[...], flat, ((1,), (0,)))
+        for l, part in enumerate(cells_to_levels(grad, lev, touched)):
+            packed[pl.ds(l, slots, stride=lev), :] = part
         phase_refs(phase)[0][...] = packed[...].astype(BF16)
         send_all(phase)
 
@@ -253,9 +274,7 @@
         lines[...] = contract(pick[...], flat, ((1,), (0,)))
         found = jnp.zeros((slots * lev, touched), F32)
         for h in range(groups):
-            part = jnp.take_along_axis(
-                lines[:, h * 128 : (h + 1) * 128], col_lo[...], axis=1, mode="promise_in_bounds"
-            )
+            part = lanes(lines[:, h * 128 : (h + 1) * 128], col_lo[...])
             found = jnp.where(col_hi[...] == h, part, found)
         phase_refs(phase)[0][...] = found.astype(BF16)
         send_all(phase)
@@ -263,10 +282,8 @@
     def observe(phase):
         recv_all(phase)
         packed[...] = phase_refs(phase)[1][...].astype(F32)
-        cells = jnp.concatenate(
-            [packed[pl.ds(l, slots, stride=lev), :] for l in range(lev)], axis=1
-        ).astype(BF16)
-        cells = contract(cells, perm[...], ((1,), (0,))).astype(BF16)
+        by_level = [packed[pl.ds(l, slots, stride=lev), :] for l in range(lev)]
+        cells = levels_to_cells(by_level, lev, touched).astype(BF16)
         flat = jac[...].reshape(tiles * jac.shape[1], jac.shape[2])
         seen = contract(cells, flat, ((1,), (1,)))
         for t in range(tiles):
@@ -295,12 +312,12 @@
                 lines[here, pl.ds(h * 128, 128)] = line[h * lev : (h + 1) * lev]
             return c
 
-        def eight(s, c):
-            for u in range(8):
-                slot_lines(8 * s + u, c)
+        def several(s, c):
+            for u in range(16):
+                slot_lines(16 * s + u, c)
             return c
 
-        lax.fori_loop(0, slots // 8, eight, 0)
+        lax.fori_loop(0, slots // 16, several, 0)
         whole = lines[...]
         high = whole.astype(BF16)
         low = (whole - high.astype(F32)).astype(BF16)
@@ -313,9 +330,6 @@
     field_0.wait()
     halo_out(0)
 
-    cells_all = touched * lev
-    perm_t[...] = reorder(cells_all, lev, BF16)
-    perm[...] = reorder(cells_all, touched, BF16)
     obs_dual[...] = dobs_in[0].astype(F32)
     loads["jac"].wait()
     adjoint_out(1)
@@ -476,21 +490,29 @@
 
 
 def deliver(*refs):
-    count = (len(refs) - 1) // 2
-    sources, targets, sem = refs[:count], refs[count : 2 * count], refs[-1]
-    copies = []
-    for src, dst in zip(sources, targets):
-        for part in range(sem.shape[1]) if src.shape[1] == sem.shape[1] else (None,):
-            here = slice(None) if part is None else pl.ds(part, 1)
-            copies.append(
-                pltpu.make_async_copy(
-                    src.at[:, here], dst.at[:, here], sem.at[len(copies) // sem.shape[1], part or 0]
+    count = (len(refs) - 2) // 3
+    sources, targets, held = (refs[i * count : (i + 1) * count] for i in range(3))
+    in_sem, out_sem = refs[-2:]
+    parts = in_sem.shape[1]
+    steps = []
+    for k, (src, dst, mid) in enumerate(zip(sources, targets, held)):
+        cuts = parts if len(src.shape) == 4 else 1
+        size = src.shape[1] // cuts
+        for part in range(cuts):
+            here = pl.ds(part * size, size)
+            steps.append(
+                (
+                    pltpu.make_async_copy(src.at[0, here], mid.at[here], in_sem.at[k, part]),
+                    pltpu.make_async_copy(mid.at[here], dst.at[0, here], out_sem.at[k, part]),
                 )
             )
-    for copy in copies:
-        copy.start()
-    for copy in copies:
-        copy.wait()
+    for read, write in steps:
+        read.start()
+    for read, write in steps:
+        read.wait()
+        write.start()
+    for read, write in steps:
+        write.wait()
 
 
 def on_device(*args):
@@ -520,8 +542,6 @@
         pltpu.VMEM(grid, F32),
         pltpu.VMEM(grid, F32),
         pltpu.VMEM(grid, F32),
-        pltpu.VMEM((cells, cells), BF16),
-        pltpu.VMEM((cells, cells), BF16),
         pltpu.VMEM((slots * lev, lev * rows), BF16),
         pltpu.VMEM((lev * rows, slots * lev), BF16),
         pltpu.VMEM((slots * lev, width), F32),
@@ -569,7 +589,7 @@
         out_shape=tuple(jax.ShapeDtypeStruct(r.shape, r.dtype) for r in results),
         in_specs=[hbm] * 3,
         out_specs=(hbm,) * 3,
-        scratch_shapes=[dma((3, lev))],
+        scratch_shapes=[pltpu.VMEM(r.shape[1:], r.dtype) for r in results] + [dma((3, 4))] * 2,
         compiler_params=pltpu.CompilerParams(vmem_limit_bytes=60 * 2**20),
         name="deliver",
     )(*results)

time: 105 us -> 41 us (0.39)
  Pallas kernels: 104 us -> 40 us
    pallas_call x1, Pallas kernels: 65.1 us -> 2.47 us  [on_device(): pl.pallas_call(deliver, out_shape=tuple((jax.ShapeDtypeStruct(r.shape, r....]
    pallas_call x1, Pallas kernels: 38.7 us -> 37.5 us  [on_device(): pl.pallas_call(functools.partial(kernel, n, cap), out_shape=(jax.ShapeDty...]
where the time goes in v3:
time: 41 us; the launch traced here: 40.6 us
  Pallas kernels  40 us (98%)
  between operations  0.64 us (2%)
    pallas_call x1, Pallas kernels, on_device(): pl.pallas_call(functools.partial(kernel, n, cap), out_shape=(jax.ShapeDty...  37.5 us
    pallas_call x1, Pallas kernels, on_device(): pl.pallas_call(deliver, out_shape=tuple((jax.ShapeDtypeStruct(r.shape, r....  2.47 us

profile of v3, /device:TPU:0, one launch (start us, length us, event | category | flops | bytes accessed | tf_op | source)
XLA Modules:
  0.0 40.6 jit_solution(4253488177838387496)
XLA Ops:
  0.6 37.5 %assimilate.1 = (f32[1,8,32,1024]{3,2,1,0:T(8,128)}, f32[1,16,128]{2,1,0:T(8,128)}, f32[1,8,32,1024]{3,2,1,0:T(8,128)}) custom-call(f32[1,8,32,1024]{3,2,1,0:T(8,128)} %inc_in.1, f32[1,8,32,1024]{3,2,1,0:T(8,128)} %dual_in.1, bf16[1,16,128]{2,1,0:T(8,128)(2,1)} %dobs_in.1, f32[1,8,32,1024]{3,2,1,0:T(8,128)} %rhs_in.1, f32[1,8,32,1024]{3,2,1,0:T(8,128)} %err_in.1, ...), custom_call_target="tpu_custom_call" | custom-call | tf_op jit(solution)/shard_map/assimilate/pallas_call | solution.py:571
  38.1 2.5 %deliver.1 = (f32[1,8,32,1024]{3,2,1,0:T(8,128)}, f32[1,8,32,1024]{3,2,1,0:T(8,128)}, f32[1,16,128]{2,1,0:T(8,128)}) custom-call(f32[1,8,32,1024]{3,2,1,0:T(8,128)} %get-tuple-element.9.refs_0_, f32[1,8,32,1024]{3,2,1,0:T(8,128)} %get-tuple-element.10.refs_1_, f32[1,16,128]{2,1,0:T(8,128)} %get-tuple-element.11.refs_2_), custom_call_target="tpu_custom_call" | custom-call | tf_op jit(solution)/shard_map/deliver/pallas_call | solution.py:587

commit v4 on v3

--- a/solution.py
+++ b/solution.py
@@ -285,9 +285,9 @@
         by_level = [packed[pl.ds(l, slots, stride=lev), :] for l in range(lev)]
         cells = levels_to_cells(by_level, lev, touched).astype(BF16)
         flat = jac[...].reshape(tiles * jac.shape[1], jac.shape[2])
-        seen = contract(cells, flat, ((1,), (1,)))
+        seen = contract(flat, cells, ((1,), (1,)))
         for t in range(tiles):
-            mine = jnp.where(slot_row == slot_of[t], seen[:, t * touched : (t + 1) * touched], 0.0)
+            mine = jnp.where(slot_row == slot_of[t], seen[t * touched : (t + 1) * touched].T, 0.0)
             image[pl.ds(t, 1), :] = jnp.sum(mine, axis=0, keepdims=True)
         variance = ovar_ref[0].astype(F32)
         held = obs_dual[...]

time: 41 us -> 42 us (1.024)
  Pallas kernels: 40 us -> 41.1 us
    pallas_call x1, Pallas kernels: 37.5 us -> 38.7 us  [on_device(): pl.pallas_call(functools.partial(kernel, n, cap), out_shape=(jax.ShapeDty...]
where the time goes in v4:
time: 42 us; the launch traced here: 41.8 us
  Pallas kernels  41.1 us (98%)
  between operations  0.64 us (2%)
    pallas_call x1, Pallas kernels, on_device(): pl.pallas_call(functools.partial(kernel, n, cap), out_shape=(jax.ShapeDty...  38.7 us
    pallas_call x1, Pallas kernels, on_device(): pl.pallas_call(deliver, out_shape=tuple((jax.ShapeDtypeStruct(r.shape, r....  2.47 us

profile of v4, /device:TPU:0, one launch (start us, length us, event | category | flops | bytes accessed | tf_op | source)
XLA Modules:
  0.0 41.8 jit_solution(15816312397610847601)
XLA Ops:
  0.6 38.7 %assimilate.1 = (f32[1,8,32,1024]{3,2,1,0:T(8,128)}, f32[1,16,128]{2,1,0:T(8,128)}, f32[1,8,32,1024]{3,2,1,0:T(8,128)}) custom-call(f32[1,8,32,1024]{3,2,1,0:T(8,128)} %inc_in.1, f32[1,8,32,1024]{3,2,1,0:T(8,128)} %dual_in.1, bf16[1,16,128]{2,1,0:T(8,128)(2,1)} %dobs_in.1, f32[1,8,32,1024]{3,2,1,0:T(8,128)} %rhs_in.1, f32[1,8,32,1024]{3,2,1,0:T(8,128)} %err_in.1, ...), custom_call_target="tpu_custom_call" | custom-call | tf_op jit(solution)/shard_map/assimilate/pallas_call | solution.py:571
  39.3 2.5 %deliver.1 = (f32[1,8,32,1024]{3,2,1,0:T(8,128)}, f32[1,8,32,1024]{3,2,1,0:T(8,128)}, f32[1,16,128]{2,1,0:T(8,128)}) custom-call(f32[1,8,32,1024]{3,2,1,0:T(8,128)} %get-tuple-element.9.refs_0_, f32[1,8,32,1024]{3,2,1,0:T(8,128)} %get-tuple-element.10.refs_1_, f32[1,16,128]{2,1,0:T(8,128)} %get-tuple-element.11.refs_2_), custom_call_target="tpu_custom_call" | custom-call | tf_op jit(solution)/shard_map/deliver/pallas_call | solution.py:587
